TPU v7x, 1024 devices: a whole 4x4x32 slice. The times are simulated.
1024 devices in a mesh: expert: 16 (over y, x), tensor: 64 (over z, core).
Axes of the slice: x: 4, y: 4, z: 32, core: 2. Of those that a mesh axis runs over, the one named last changes fastest.
Arguments:
- tokens: bfloat16 [2048, 7168], P('expert', 'tensor'), may hold values from -6 to 6
- gate_weights: bfloat16 [2048, 1], P('expert'), may hold values from 0.099609375 to 1
- expert_ids: int32 [2048, 1], P('expert'), may hold values from 0 to 15; in each aligned block of 128 rows (0 to 127, 128 to 255, ...) at most 12 rows name the same one
- w_gate: bfloat16 [16, 7168, 2048], P('expert', 'tensor'), may hold values from -0.0625 to 0.0625
- w_up: bfloat16 [16, 7168, 2048], P('expert', 'tensor'), may hold values from -0.0625 to 0.0625
- w_down: bfloat16 [16, 2048, 7168], P('expert', None, 'tensor'), may hold values from -0.125 to 0.125
- grad_out: bfloat16 [2048, 7168], P('expert', 'tensor'), may hold values from -6 to 6
Outputs:
- mixed: bfloat16 [2048, 7168], P('expert', 'tensor')
- grad_tokens: bfloat16 [2048, 7168], P('expert', 'tensor')
- grad_w_gate: bfloat16 [16, 7168, 2048], P('expert', 'tensor')
- grad_w_up: bfloat16 [16, 7168, 2048], P('expert', 'tensor')
- grad_w_down: bfloat16 [16, 2048, 7168], P('expert', None, 'tensor')
Inputs may be any that keep to these rules, and one draw needn't show every extreme that they name: `expert_ids`: the 1 expert of a token differ. The tokens of one expert index (aligned blocks of 128 rows) name one expert at most 12 times, a bound that some block reaches.
All inputs are finite; a program needn't handle non-finite values.
Results may differ from a plain program's by a relative error of at most 0.0058.
Values may be sent and summed in bfloat16 or wider, within the bound.
A program may use at most 32 MiB of HBM per device.

v0:
```python
import jax
import jax.numpy as jnp
from jax import lax
from jax.sharding import PartitionSpec as P


def swapped(x, axis, stride):
    return lax.ppermute(x, axis, [(i, i ^ 1 << stride) for i in range(lax.axis_size(axis))])


def pairwise_move(stacked, own_index, members):
    partner_order = jnp.bitwise_xor(own_index, jnp.arange(members, dtype=jnp.int32))
    holding = jnp.take(stacked, partner_order, axis=0)
    levels = members.bit_length() - 1
    for level in range(levels):
        stride = 1 << level
        halves = holding.reshape((members // (2 * stride), 2, stride) + holding.shape[1:])
        received = swapped(halves[:, 1], "expert", level)
        holding = jnp.stack([halves[:, 0], received], axis=1).reshape(holding.shape)
    return jnp.take(holding, partner_order, axis=0)


def spread_units(function, share):
    return lax.psum_scatter(
        function(jnp.int32(0), share * lax.axis_size("tensor")),
        "tensor",
        scatter_dimension=0,
        tiled=True,
    )


def local(tokens, gate_weights, expert_ids, w_gate, w_up, w_down, grad_out):
    members = lax.axis_size("expert")
    tensor_count = lax.axis_size("tensor")
    own_index = lax.axis_index("expert")
    tok_rows = tokens.shape[0]
    routes = expert_ids.shape[1]
    width = tokens.shape[1]
    slot = 3 * routes * tok_rows // (2 * members)
    total = members * slot
    flat_ids = expert_ids.reshape(-1)
    counted = (flat_ids[:, None] == jnp.arange(members, dtype=jnp.int32)[None, :]).astype(jnp.int32)
    ranks = jnp.cumsum(counted, axis=0) - 1
    position = jnp.sum(counted * ranks, axis=1)
    target = (flat_ids * slot + position).reshape(tok_rows, routes)
    matched = target[None, :, :] == jnp.arange(total, dtype=jnp.int32)[:, None, None]
    place = jnp.sum(matched.astype(jnp.float32), axis=2).astype(jnp.bfloat16)
    weighted = jnp.sum(
        jnp.where(matched, gate_weights.astype(jnp.float32)[None], 0.0), axis=2
    ).astype(jnp.bfloat16)
    x_slots = jnp.dot(place, tokens, preferred_element_type=jnp.float32).astype(jnp.bfloat16)
    dy_slots = jnp.dot(weighted, grad_out, preferred_element_type=jnp.float32).astype(jnp.bfloat16)
    outgoing = jnp.stack(
        [x_slots.reshape(members, slot, width), dy_slots.reshape(members, slot, width)], axis=1
    )
    arrived = pairwise_move(outgoing, own_index, members)
    x_rows = arrived[:, 0].reshape(total, width)
    dy_rows = arrived[:, 1].reshape(total, width)
    weight_gate = w_gate[0]
    weight_up = w_up[0]
    weight_down = w_down[0]
    share = weight_gate.shape[1] // tensor_count

    def gate_terms(start, count):
        gate_part = lax.dot_general(
            weight_gate, x_rows, (((0,), (1,)), ((), ())), preferred_element_type=jnp.float32
        )
        up_part = lax.dot_general(
            weight_up, x_rows, (((0,), (1,)), ((), ())), preferred_element_type=jnp.float32
        )
        return jnp.concatenate([gate_part, up_part], axis=1)

    summed = spread_units(gate_terms, share)
    gate_t = summed[:, :total]
    up_t = summed[:, total:]
    sigma = jax.nn.sigmoid(gate_t)
    active = gate_t * sigma
    hidden_t = (active * up_t).astype(jnp.bfloat16)
    hidden_full = lax.all_gather(hidden_t, "tensor", axis=0, tiled=True)
    out_rows = lax.dot_general(
        hidden_full, weight_down, (((0,), (0,)), ((), ())), preferred_element_type=jnp.float32
    ).astype(jnp.bfloat16)
    out_slots = out_rows.reshape(members, slot, width)
    out_back = lax.all_to_all(out_slots, "expert", split_axis=0, concat_axis=0, tiled=True)

    def grad_terms(start, count):
        return lax.dot_general(
            weight_down, dy_rows, (((1,), (1,)), ((), ())), preferred_element_type=jnp.float32
        )

    d_hidden = spread_units(grad_terms, share)
    d_gate_t = (d_hidden * up_t * sigma * (1.0 + gate_t * (1.0 - sigma))).astype(jnp.bfloat16)
    d_up_t = (d_hidden * active).astype(jnp.bfloat16)
    d_gate_full, d_up_full = (
        lax.all_gather(d_gate_t, "tensor", axis=0, tiled=True),
        lax.all_gather(d_up_t, "tensor", axis=0, tiled=True),
    )
    back_rows = (
        lax.dot_general(
            d_gate_full, weight_gate, (((0,), (1,)), ((), ())), preferred_element_type=jnp.float32
        )
        + lax.dot_general(
            d_up_full, weight_up, (((0,), (1,)), ((), ())), preferred_element_type=jnp.float32
        )
    ).astype(jnp.bfloat16)
    grad_w_gate = lax.dot_general(
        x_rows, d_gate_full, (((0,), (1,)), ((), ())), preferred_element_type=jnp.float32
    ).astype(jnp.bfloat16)[None]
    grad_w_up = lax.dot_general(
        x_rows, d_up_full, (((0,), (1,)), ((), ())), preferred_element_type=jnp.float32
    ).astype(jnp.bfloat16)[None]
    grad_w_down = lax.dot_general(
        hidden_full, dy_rows, (((1,), (0,)), ((), ())), preferred_element_type=jnp.float32
    ).astype(jnp.bfloat16)[None]
    back_slots = back_rows.reshape(members, slot, width)
    grad_back = lax.all_to_all(back_slots, "expert", split_axis=0, concat_axis=0, tiled=True)
    mixed = lax.dot_general(
        weighted,
        out_back.reshape(total, width),
        (((0,), (0,)), ((), ())),
        preferred_element_type=jnp.float32,
    ).astype(jnp.bfloat16)
    grad_tokens = lax.dot_general(
        place,
        grad_back.reshape(total, width),
        (((0,), (0,)), ((), ())),
        preferred_element_type=jnp.float32,
    ).astype(jnp.bfloat16)
    return (mixed, grad_tokens, grad_w_gate, grad_w_up, grad_w_down)


def solution(mesh):
    in_specs = (
        P("expert", "tensor"),
        P("expert", None),
        P("expert", None),
        P("expert", "tensor", None),
        P("expert", "tensor", None),
        P("expert", None, "tensor"),
        P("expert", "tensor"),
    )
    out_specs = (
        P("expert", "tensor"),
        P("expert", "tensor"),
        P("expert", "tensor", None),
        P("expert", "tensor", None),
        P("expert", None, "tensor"),
    )
    return jax.shard_map(local, mesh=mesh, in_specs=in_specs, out_specs=out_specs, check_vma=False)
```

profile of v0, /device:TPU:1, one launch (start us, length us, event | category | flops | bytes accessed | tf_op | source)
XLA Modules:
  0.0 681.4 jit_solution(2941657934072375863)
XLA Ops:
  9.7 0.9 convolution_convert_fusion.4
  12.4 3.9 collective-permute-start
  16.4 1.4 collective-permute-done
  18.0 4.9 collective-permute-start.1
  22.9 1.5 collective-permute-done.1
  24.9 3.4 collective-permute-start.2
  28.4 1.5 collective-permute-done.2
  30.1 5.0 collective-permute-start.3
  35.0 1.5 collective-permute-done.3
  38.5 1.8 copy.70
  40.4 0.9 copy-done.1
  42.1 2.0 pad_maximum_fusion
  44.1 3.5 copy.68
  47.7 213.5 %reduce-scatter.9.cloned.1.call-done = f32[32,192]{1,0:T(8,128)} async-done(((f32[2048,192]{1,0:T(8,128)}), f32[32,192]{1,0:T(8,128)}) %reduce-scatter.9.cloned.1.call-update) | async-done | bytes 24592 | tf_op jit(solution)/shard_map/reduce_scatter | solution.py:24
  261.1 212.8 %reduce-scatter.7.cloned.1.call-done = f32[32,384]{1,0:T(8,128)} async-done(((f32[2048,384]{1,0:T(8,128)}), f32[32,384]{1,0:T(8,128)}) %reduce-scatter.7.cloned.1.call-update) | async-done | bytes 49168 | tf_op jit(solution)/shard_map/reduce_scatter | solution.py:24
  474.8 59.0 %all_gather.10 = bf16[2048,192]{1,0:T(8,128)(2,1)S(1)} all-gather(bf16[32,192]{1,0:T(8,128)(2,1)S(1)} %get-tuple-element.17), channel_id=1, replica_groups=mesh['expert'=16,'tensor'=64] {'tensor'}, dimensions={0}, use_global_device_ids=true | all-gather | bytes 798720 | tf_op jit(solution)/shard_map/all_gather | solution.py:95
  534.3 1.2 fusion
  535.6 57.9 %all_gather.11 = bf16[2048,192]{1,0:T(8,128)(2,1)S(1)} all-gather(bf16[32,192]{1,0:T(8,128)(2,1)S(1)} %get-tuple-element.16), channel_id=1, replica_groups=mesh['expert'=16,'tensor'=64] {'tensor'}, dimensions={0}, use_global_device_ids=true | all-gather | bytes 798720 | tf_op jit(solution)/shard_map/all_gather | solution.py:96
  593.5 1.2 fusion.1
  595.8 6.5 all-to-all-start.1
  602.4 55.5 %all_gather.9 = bf16[2048,192]{1,0:T(8,128)(2,1)S(1)} all-gather(bf16[32,192]{1,0:T(8,128)(2,1)S(1)} %get-tuple-element.18), channel_id=1, replica_groups=mesh['expert'=16,'tensor'=64] {'tensor'}, dimensions={0}, use_global_device_ids=true | all-gather | bytes 798720 | tf_op jit(solution)/shard_map/all_gather | solution.py:79
  658.4 1.2 fusion.2
  660.3 6.9 %all-to-all-start = ((bf16[16,12,112]{2,1,0:T(8,128)(2,1)}), bf16[16,12,112]{2,1,0:T(8,128)(2,1)S(1)}, u32[]{:S(2)}, u32[]{:S(2)}) async-start(bf16[16,12,112]{2,1,0:T(8,128)(2,1)} %reshape.182), calls=%async_computation | async-start | bytes 131072 | tf_op jit(solution)/shard_map/all_to_all | solution.py:84
  668.0 5.7 all-to-all-done
  (57 shorter events, 13.2 us)
Async XLA Ops:
  7.2 34.5 %copy-start = (bf16[1,112,2048]{2,1,0:T(8,128)(2,1)S(1)}, bf16[1,112,2048]{2,1,0:T(8,128)(2,1)}, u32[]{:S(2)}) copy-start(bf16[1,112,2048]{2,1,0:T(8,128)(2,1)} %param.12) | copy-start | bytes 1376260
  7.2 253.9 %reduce-scatter.9.cloned.1.call-start = ((), (), s32[]{:S(2)}) async-start(), calls=%async_computation.5 | async-start | bytes 2129920 | tf_op jit(solution)/shard_map/reduce_scatter | solution.py:24
  12.4 5.4 collective-permute-start
  17.8 20.3 %copy-start.2 = (bf16[1,2048,112]{1,2,0:T(8,128)(2,1)S(1)}, bf16[1,2048,112]{1,2,0:T(8,128)(2,1)}, u32[]{:S(2)}) copy-start(bf16[1,2048,112]{1,2,0:T(8,128)(2,1)} %param.14) | copy-start | bytes 1376260
  18.0 6.4 collective-permute-start.1
  24.9 4.9 collective-permute-start.2
  30.1 6.5 collective-permute-start.3
  40.3 1.0 copy-start.1
  40.4 433.6 %reduce-scatter.7.cloned.1.call-start = ((), (), s32[]{:S(2)}) async-start(), calls=%async_computation.4 | async-start | bytes 3194880 | tf_op jit(solution)/shard_map/reduce_scatter | solution.py:24
  595.8 64.4 %all-to-all-start.1 = ((bf16[16,12,112]{2,1,0:T(8,128)(2,1)}), bf16[16,12,112]{2,1,0:T(8,128)(2,1)S(1)}, u32[]{:S(2)}, u32[]{:S(2)}) async-start(bf16[16,12,112]{2,1,0:T(8,128)(2,1)} %reshape.184), calls=%async_computation.1 | async-start | bytes 131072 | tf_op jit(solution)/shard_map/all_to_all | solution.py:116
  657.9 15.9 %copy-start.3 = (bf16[128,1]{0,1:T(2,128)(2,1)S(1)}, bf16[128,1]{0,1:T(2,128)(2,1)}, u32[]{:S(2)}) copy-start(bf16[128,1]{0,1:T(2,128)(2,1)} %param.10) | copy-start | bytes 772
  660.3 13.4 %all-to-all-start = ((bf16[16,12,112]{2,1,0:T(8,128)(2,1)}), bf16[16,12,112]{2,1,0:T(8,128)(2,1)S(1)}, u32[]{:S(2)}, u32[]{:S(2)}) async-start(bf16[16,12,112]{2,1,0:T(8,128)(2,1)} %reshape.182), calls=%async_computation | async-start | bytes 131072 | tf_op jit(solution)/shard_map/all_to_all | solution.py:84
Sparse Core Ops, SparseCore 0:
  40.5 220.5 reduce-scatter.8
  264.9 209.0 reduce-scatter.6
where the time goes:
time: 682 us; the launch traced here: 681 us
  waiting for transfers between devices  438 us (64%)
  blocking collectives  172 us (25%)
  starting transfers between devices  30.7 us (5%)
  between operations  14.4 us (2%)
  local copies, waits for them, and re-layouts  10.1 us (1%)
  matrix products  9.64 us (1%)
    reduce_scatter x2, waiting for transfers between devices, spread_units(): lax.psum_scatter(function(jnp.int32(0), share * lax.axis_size('tensor')),...  426 us
    all_gather x1, blocking collectives, local(): lax.all_gather(d_gate_t, 'tensor', axis=0, tiled=True)  59 us
    all_gather x1, blocking collectives, local(): lax.all_gather(d_up_t, 'tensor', axis=0, tiled=True)  57.9 us
    all_gather x1, blocking collectives, local(): hidden_full = lax.all_gather(hidden_t, 'tensor', axis=0, tiled=True)  55.5 us
    ppermute x4, starting transfers between devices, swapped(): lax.ppermute(x, axis, [(i, i ^ 1 << stride) for i in range(lax.axis_size(...  17.2 us
  transfers between devices with their start and end apart: 8, of which 7 were waited for; matrix products, arithmetic and copies ran while one was open for 1% of the time, Pallas kernels for 0%

commit v1 on v0

v1 whole, which is shorter than its diff:
```python
import functools

import jax
import jax.numpy as jnp
from jax import lax
from jax.experimental import pallas as pl
from jax.experimental.pallas import tpu as pltpu
from jax.sharding import PartitionSpec as P

MESH = pl.DeviceIdType.MESH
F32 = jnp.float32
BF16 = jnp.bfloat16
LANES = 128
FULL = 256
TAIL = 64
UNITS = 32
FOLD = UNITS + UNITS // 2
KINDS = 3
SENT = F32

NT = (((1,), (1,)), ((), ()))
NN = (((1,), (0,)), ((), ()))


def dot(a, b, dims=NN):
    return lax.dot_general(a, b, dims, preferred_element_type=F32)


def padded(x):
    return jnp.concatenate([x, jnp.zeros((LANES - x.shape[0], x.shape[1]), x.dtype)], axis=0)


def iota(shape, dim):
    return lax.broadcasted_iota(jnp.int32, shape, dim)


def kernel(
    experts, chips,
    tok_ref, g_ref, id_ref, wg_ref, wu_ref, wd_ref, dy_ref,
    mixed_ref, gtok_ref, gwg_ref, gwu_ref, gwd_ref,
    out_slots, in_slots, ret_slots, back_slots, xt, wt, wm, part, gath, acc_out, acc_back,
    disp_s, disp_r, ret_s, ret_r, mate_s, mate_r, rs_s, rs_r, ag_s, ag_r, am_s, am_r,
):
    e = lax.axis_index("expert")
    t = lax.axis_index("tensor")
    z, c = lax.div(t, 2), lax.rem(t, 2)
    pad = FULL // experts
    slot = 192 // experts
    depth = wg_ref.shape[0]
    half = chips // 2
    weights = (wg_ref, wu_ref, wd_ref)

    def at_chip(k):
        return lax.rem(k + 2 * chips, chips)

    up_id = {"tensor": 2 * at_chip(z + 1) + c}
    down_id = {"tensor": 2 * at_chip(z - 1) + c}
    mate_id = {"tensor": 2 * z + 1 - c}
    ring = (up_id, down_id)

    barrier = pltpu.get_barrier_semaphore()
    for peer in (up_id, down_id, mate_id):
        pl.semaphore_signal(barrier, inc=1, device_id=peer, device_id_type=MESH)

    def greet(i, _):
        pl.semaphore_signal(
            barrier, inc=1, device_id={"expert": lax.rem(e + i, experts)}, device_id_type=MESH
        )
        return 0

    lax.fori_loop(1, experts, greet, 0)

    ids = id_ref[...]
    here = (iota((experts, LANES), 0) == ids).astype(F32)
    before = (iota((LANES, LANES), 0) < iota((LANES, LANES), 1)).astype(BF16)
    ranks = dot(here.astype(BF16), before)
    position = jnp.sum(here * ranks, axis=0, keepdims=True)
    target = ids * pad + position.astype(jnp.int32)
    matched = iota((FULL, LANES), 0) == target
    place = jnp.where(matched, 1.0, 0.0).astype(BF16)
    weighted = jnp.where(matched, g_ref[...].astype(F32), 0.0).astype(BF16)
    x_slots = dot(place, padded(tok_ref[...]), NT).astype(BF16)
    dy_slots = dot(weighted, padded(dy_ref[...]), NT).astype(BF16)
    out_slots[:, :, :LANES] = x_slots.reshape(experts, pad, LANES)
    out_slots[:, :, LANES:] = dy_slots.reshape(experts, pad, LANES)

    pl.semaphore_wait(barrier, experts + 2)

    def leave(src, dst, send, recv, i):
        peer = lax.rem(e + i, experts)
        return pltpu.make_async_remote_copy(
            src_ref=src.at[peer], dst_ref=dst.at[e], send_sem=send.at[i], recv_sem=recv.at[i],
            device_id={"expert": peer}, device_id_type=MESH,
        )

    def arrive(src, dst, send, recv, i):
        origin = lax.rem(e - i + experts, experts)
        return pltpu.make_async_remote_copy(
            src_ref=src.at[origin], dst_ref=dst.at[origin], send_sem=send.at[i],
            recv_sem=recv.at[i], device_id={"expert": origin}, device_id_type=MESH,
        )

    def all_start(src, dst, send, recv):
        def body(i, _):
            leave(src, dst, send, recv, i).start()
            return 0

        lax.fori_loop(1, experts, body, 0)
        dst[e] = src[e]

    def all_wait(src, dst, send, recv):
        def body(i, _):
            arrive(src, dst, send, recv, i).wait_recv()
            return 0

        lax.fori_loop(1, experts, body, 0)

    def all_sent(src, dst, send, recv):
        def body(i, _):
            leave(src, dst, send, recv, i).wait_send()
            return 0

        lax.fori_loop(1, experts, body, 0)

    dispatch = (out_slots, in_slots, disp_s, disp_r)
    all_start(*dispatch)

    def mate_weights(k):
        return pltpu.make_async_remote_copy(
            src_ref=wt.at[k, :, 1 - c], dst_ref=wm.at[k], send_sem=mate_s.at[k],
            recv_sem=mate_r.at[k], device_id=mate_id, device_id_type=MESH,
        )

    for k in range(KINDS):
        def turn(i, _, k=k):
            cols = pl.ds(pl.multiple_of(i * LANES, LANES), LANES)
            block = padded(weights[k][:, cols]).T
            wt[k, pl.ds(2 * i, 2)] = block.reshape(2, 2, UNITS, LANES)
            return 0

        lax.fori_loop(0, chips // 2, turn, 0)
        mate_weights(k).start()

    s_i, r_i = iota((FULL, FULL), 0), iota((FULL, FULL), 1)
    inner = lax.bitwise_and(s_i, pad - 1)
    first = lax.shift_right_logical(s_i, pad.bit_length() - 1) * slot
    r_of = jnp.where(r_i >= 192, r_i - TAIL, r_i)
    valid = inner < slot
    spread = jnp.where(valid & (r_of - first == inner), 1.0, 0.0).astype(BF16)
    gather = jnp.where(valid & (r_i - first == inner), 1.0, 0.0).astype(BF16)

    all_wait(*dispatch)
    arrived = in_slots[...].reshape(FULL, FULL)
    panels = dot(arrived.T, spread).astype(BF16)
    xt[0, 0] = panels[:LANES]
    xt[1, 0] = panels[LANES:]
    mate_rows = pltpu.make_async_remote_copy(
        src_ref=xt.at[:, 0], dst_ref=xt.at[:, 1], send_sem=mate_s.at[KINDS],
        recv_sem=mate_r.at[KINDS], device_id=mate_id, device_id_type=MESH,
    )
    mate_rows.start()
    for k in range(KINDS):
        mate_weights(k).wait_recv()
    mate_rows.wait_recv()

    low = iota((UNITS // 2, LANES), 1) < TAIL

    def partial(chip):
        sums = []
        for k in range(KINDS):
            lhs = jnp.concatenate([wt[k, chip, c], wm[k, chip]], axis=1)
            r = dot(lhs, xt[0 if k < 2 else 1].reshape(FULL, FULL))
            tail = jnp.where(low, r[: UNITS // 2, LANES:], r[UNITS // 2 :, LANES:])
            sums.append(jnp.concatenate([r[:, :LANES], tail], axis=0))
        return sums

    def hop(way, s, k):
        return pltpu.make_async_remote_copy(
            src_ref=part.at[way, s, k], dst_ref=part.at[way, s + 1, k],
            send_sem=rs_s.at[way, s, k], recv_sem=rs_r.at[way, s, k],
            device_id=ring[way], device_id_type=MESH,
        )

    mine = partial(at_chip(z + half))
    for k in range(KINDS):
        part[0, 0, k] = mine[k].astype(SENT)
        hop(0, 0, k).start()
    mine = partial(at_chip(z - half + 1))
    for k in range(KINDS):
        part[1, 0, k] = mine[k].astype(SENT)
        hop(1, 0, k).start()

    def rs_step(i, _):
        ups = partial(at_chip(z + half - i))
        for k in range(KINDS):
            hop(0, i - 1, k).wait_recv()
            part[0, i, k] = (part[0, i, k].astype(F32) + ups[k]).astype(SENT)
            hop(0, i, k).start()

        @pl.when(i > 1)
        def _():
            downs = partial(at_chip(z - half + i))
            for k in range(KINDS):
                hop(1, i - 2, k).wait_recv()
                part[1, i - 1, k] = (part[1, i - 1, k].astype(F32) + downs[k]).astype(SENT)
                hop(1, i - 1, k).start()

        return 0

    lax.fori_loop(1, half, rs_step, 0)
    own = partial(z)
    total = []
    for k in range(KINDS):
        hop(0, half - 1, k).wait_recv()
        hop(1, half - 2, k).wait_recv()
        total.append(part[0, half, k].astype(F32) + part[1, half - 1, k].astype(F32) + own[k])
    gate, up, d_hidden = total
    sigma = jax.nn.sigmoid(gate)
    active = gate * sigma
    gath[z, c, 0] = (active * up).astype(BF16)
    gath[z, c, 1] = (d_hidden * up * sigma * (1.0 + gate * (1.0 - sigma))).astype(BF16)
    gath[z, c, 2] = (d_hidden * active).astype(BF16)

    def lap(way, s, k):
        origin = at_chip(z - s) if way == 0 else at_chip(z + s)
        return pltpu.make_async_remote_copy(
            src_ref=gath.at[origin, c, k], dst_ref=gath.at[origin, c, k],
            send_sem=ag_s.at[way, s, k], recv_sem=ag_r.at[way, s, k],
            device_id=ring[way], device_id_type=MESH,
        )

    def lap_in(way, s, k):
        origin = at_chip(z - s - 1) if way == 0 else at_chip(z + s + 1)
        return pltpu.make_async_remote_copy(
            src_ref=gath.at[origin, c, k], dst_ref=gath.at[origin, c, k],
            send_sem=ag_s.at[way, s, k], recv_sem=ag_r.at[way, s, k],
            device_id=ring[way], device_id_type=MESH,
        )

    def across(origin, k):
        return pltpu.make_async_remote_copy(
            src_ref=gath.at[origin, c, k], dst_ref=gath.at[origin, c, k],
            send_sem=am_s.at[origin, k], recv_sem=am_r.at[origin, k],
            device_id=mate_id, device_id_type=MESH,
        )

    def across_in(origin, k):
        return pltpu.make_async_remote_copy(
            src_ref=gath.at[origin, 1 - c, k], dst_ref=gath.at[origin, 1 - c, k],
            send_sem=am_s.at[origin, k], recv_sem=am_r.at[origin, k],
            device_id=mate_id, device_id_type=MESH,
        )

    for k in range(KINDS):
        lap(0, 0, k).start()
        lap(1, 0, k).start()
        across(z, k).start()

    acc_out[...] = jnp.zeros_like(acc_out)
    acc_back[...] = jnp.zeros_like(acc_back)
    odd = lax.rem(z, 2)
    low2 = iota((UNITS // 2, LANES), 1) < TAIL
    zero2 = jnp.zeros((UNITS // 2, LANES), BF16)

    def use(pair):
        first_chip = at_chip(z - odd + 2 * pair)
        for i in range(2):
            for k in range(KINDS):
                across_in(first_chip + i, k).wait_recv()
        panel = []
        for k in range(KINDS):
            rows = []
            for i in range(2):
                for core in range(2):
                    v = gath[first_chip + i, core, k]
                    tail = v[UNITS:]
                    rows.append(
                        jnp.concatenate(
                            [
                                v[:UNITS],
                                jnp.concatenate(
                                    [jnp.where(low2, tail, zero2), jnp.where(low2, zero2, tail)],
                                    axis=0,
                                ),
                            ],
                            axis=1,
                        )
                    )
            panel.append(jnp.concatenate(rows, axis=0))
        hidden, d_gate, d_up = panel
        cols = pl.ds(pl.multiple_of(first_chip * 2 * UNITS, LANES), LANES)
        acc_out[...] += dot(wd_ref[:, cols], hidden)
        acc_back[...] += dot(wg_ref[:, cols], d_gate) + dot(wu_ref[:, cols], d_up)
        x_panel, dy_panel = xt[0, 0][:depth], xt[1, 0][:depth]
        gwg_ref[:, cols] = dot(x_panel, d_gate, NT).astype(BF16)
        gwu_ref[:, cols] = dot(x_panel, d_up, NT).astype(BF16)
        gwd_ref[:, cols] = dot(dy_panel, hidden, NT).astype(BF16)

    def forward(s):
        for k in range(KINDS):
            lap_in(0, s, k).wait_recv()

            @pl.when(s < half - 1)
            def _():
                lap(0, s + 1, k).start()

            across(at_chip(z - s - 1), k).start()

            @pl.when(s < half - 1)
            def _():
                lap_in(1, s, k).wait_recv()

                @pl.when(s < half - 2)
                def _():
                    lap(1, s + 1, k).start()

                across(at_chip(z + s + 1), k).start()

    forward(0)
    forward(1)

    def ag_step(j, _):
        forward(2 * j)
        use(j - 1 + odd)
        forward(2 * j + 1)
        use(odd - j)
        return 0

    lax.fori_loop(1, half // 2, ag_step, 0)
    use(half // 2 - 1 + odd)
    use(odd - half // 2)

    def folded(acc):
        a = acc[:, LANES:]
        whole = jnp.concatenate([acc[:, :LANES], a + pltpu.roll(a, TAIL, 1)], axis=1)
        return padded(whole.astype(BF16))

    out_rows = dot(gather, folded(acc_out[...]), NT).astype(BF16)
    ret_slots[:, :, :LANES] = out_rows.reshape(experts, pad, LANES)
    back_rows = dot(gather, folded(acc_back[...]), NT).astype(BF16)
    ret_slots[:, :, LANES:] = back_rows.reshape(experts, pad, LANES)
    homeward = (ret_slots, back_slots, ret_s, ret_r)
    all_start(*homeward)

    all_sent(*dispatch)
    for k in range(KINDS):
        mate_weights(k).wait_send()
    mate_rows.wait_send()

    def drain(s, _):
        for k in range(KINDS):
            hop(0, s, k).wait_send()
            lap(0, s, k).wait_send()

            @pl.when(s < half - 1)
            def _():
                hop(1, s, k).wait_send()
                lap(1, s, k).wait_send()

        return 0

    lax.fori_loop(0, half, drain, 0)

    def drain_across(o, _):
        for k in range(KINDS):
            across(o, k).wait_send()
        return 0

    lax.fori_loop(0, chips, drain_across, 0)

    all_wait(*homeward)
    returned = back_slots[...].reshape(FULL, FULL).T
    mixed_ref[...] = dot(returned[:depth], weighted).astype(BF16)
    gtok_ref[...] = dot(returned[LANES : LANES + depth], place).astype(BF16)
    all_sent(*homeward)


def local(experts, chips, tokens, gate_weights, expert_ids, w_gate, w_up, w_down, grad_out):
    depth, width = w_gate.shape[1:]
    pad = FULL // experts
    half = chips // 2
    dma = pltpu.SemaphoreType.DMA
    slots = pltpu.VMEM((experts, pad, FULL), BF16)
    rows = jax.ShapeDtypeStruct((depth, LANES), BF16)
    grads = jax.ShapeDtypeStruct((depth, width), BF16)
    vmem = pl.BlockSpec(memory_space=pltpu.VMEM)
    mixed, grad_tokens, gwg, gwu, gwd = pl.pallas_call(
        functools.partial(kernel, experts, chips),
        out_shape=(rows, rows, grads, grads, grads),
        in_specs=[vmem] * 7,
        out_specs=(vmem,) * 5,
        scratch_shapes=[
            slots, slots, slots, slots,
            pltpu.VMEM((2, 2, LANES, FULL), BF16),
            pltpu.VMEM((KINDS, chips, 2, UNITS, LANES), BF16),
            pltpu.VMEM((KINDS, chips, UNITS, LANES), BF16),
            pltpu.VMEM((2, half + 1, KINDS, FOLD, LANES), SENT),
            pltpu.VMEM((chips, 2, KINDS, FOLD, LANES), BF16),
            pltpu.VMEM((depth, FULL), F32),
            pltpu.VMEM((depth, FULL), F32),
            dma((experts,)), dma((experts,)), dma((experts,)), dma((experts,)),
            dma((KINDS + 1,)), dma((KINDS + 1,)),
            dma((2, half, KINDS)), dma((2, half, KINDS)),
            dma((2, half, KINDS)), dma((2, half, KINDS)),
            dma((chips, KINDS)), dma((chips, KINDS)),
        ],
        compiler_params=pltpu.CompilerParams(
            collective_id=0, has_side_effects=True, vmem_limit_bytes=40 * 2**20
        ),
        name="routed_experts",
    )(tokens.T, gate_weights.T, expert_ids.T, w_gate[0], w_up[0], w_down[0].T, grad_out.T)
    return mixed.T, grad_tokens.T, gwg[None], gwu[None], gwd.T[None]


def solution(mesh):
    in_specs = (
        P("expert", "tensor"),
        P("expert", None),
        P("expert", None),
        P("expert", "tensor", None),
        P("expert", "tensor", None),
        P("expert", None, "tensor"),
        P("expert", "tensor"),
    )
    out_specs = (
        P("expert", "tensor"),
        P("expert", "tensor"),
        P("expert", "tensor", None),
        P("expert", "tensor", None),
        P("expert", None, "tensor"),
    )
    body = functools.partial(local, mesh.shape["expert"], mesh.shape["tensor"] // 2)
    return jax.shard_map(body, mesh=mesh, in_specs=in_specs, out_specs=out_specs, check_vma=False)
```

time: 682 us -> 152 us (0.22)
  waiting for transfers between devices: 438 us -> 0 us
  blocking collectives: 172 us -> 0 us
  Pallas kernels: 0 us -> 142 us
  starting transfers between devices: 30.7 us -> 0 us
  between operations: 14.4 us -> 0.67 us
  matrix products: 9.64 us -> 0 us
    reduce_scatter x2 -> x0, waiting for transfers between devices: 426 us -> none  [spread_units(): lax.psum_scatter(function(jnp.int32(0), share * lax.axis_size('tensor')),...]
    all_gather x3 -> x0, blocking collectives: 172 us -> none  [the longest x1 59 us: local(): lax.all_gather(d_gate_t, 'tensor', axis=0, tiled=True)]
    pallas_call x0 -> x1, Pallas kernels: none -> 142 us  [local(): pl.pallas_call(functools.partial(kernel, experts, chips), out_shape=(rows...]
    ppermute x4 -> x0, starting transfers between devices: 17.2 us -> none  [swapped(): lax.ppermute(x, axis, [(i, i ^ 1 << stride) for i in range(lax.axis_size(...]
    all_to_all x2 -> x0, starting transfers between devices: 13.4 us -> none  [the longest x1 6.89 us: local(): lax.all_to_all(out_slots, 'expert', split_axis=0, concat_axis=0, tiled=True)]
    dot_general x13 -> x0, matrix products: 9.64 us -> none  [the longest x1 1.24 us: local(): lax.dot_general(x_rows, d_gate_full, (((0,), (1,)), ((), ())), preferred_...]
  transfers between devices with their start and end apart: 8 -> 0, of which waited for: 7 -> 0; matrix products, arithmetic and copies ran while one was open for 1% -> 0% of each run, Pallas kernels for 0% -> 0%
where the time goes in v1:
time: 152 us; the launch traced here: 151 us
  Pallas kernels  142 us (93%)
  local copies, waits for them, and re-layouts  8.72 us (6%)
    pallas_call x1, Pallas kernels, local(): pl.pallas_call(functools.partial(kernel, experts, chips), out_shape=(rows...  142 us
    unnamed x19, local copies, waits for them, and re-layouts  8.72 us

profile of v1, /device:TPU:1, one launch (start us, length us, event | category | flops | bytes accessed | tf_op | source)
XLA Modules:
  0.0 151.5 jit_solution(2147830653331146549)
XLA Ops:
  0.6 0.0 copy-start.5
  0.6 0.0 copy-start.6
  0.7 0.6 copy-done.5
  1.3 0.0 copy-done.6
  1.3 0.0 copy-start
  1.3 1.0 copy-done
  2.3 0.0 copy-start.1
  2.3 1.0 copy-done.1
  3.3 0.0 copy-start.2
  3.3 1.0 copy-done.2
  4.4 0.0 copy-start.3
  4.4 0.7 copy-done.3
  5.1 0.0 copy-start.4
  5.1 0.7 copy-done.4
  5.9 142.1 %routed_experts.1 = (bf16[112,128]{1,0:T(8,128)(2,1)S(1)}, bf16[112,128]{1,0:T(8,128)(2,1)S(1)}, bf16[112,2048]{1,0:T(8,128)(2,1)S(1)}, bf16[112,2048]{1,0:T(8,128)(2,1)S(1)}, bf16[112,2048]{1,0:T(8,128)(2,1)S(1)}) custom-call(bf16[112,128]{1,0:T(8,128)(2,1)S(1)} %bitcast.24, bf16[1,128]{1,0:T(2,128)(2,1)S(1)} %bitcast.26, s32[1,128]{1,0:T(1,128)S(1)} %bitcast.27, ...), custom_call_target="tpu_custom_call" | custom-call | tf_op jit(solution)/shard_map/routed_experts/pallas_call | solution.py:387
  148.0 0.6 copy.17
  148.6 0.6 copy.18
  149.2 0.8 copy.19
  150.0 0.8 copy.20
  150.7 0.8 copy.21
Async XLA Ops:
  0.6 0.7 copy-start.5
  0.6 0.7 copy-start.6
  1.3 1.0 copy-start
  2.3 1.0 copy-start.1
  3.3 1.0 copy-start.2
  4.4 0.7 copy-start.3
  5.1 0.7 copy-start.4

commit v2 on v1

--- a/solution.py
+++ b/solution.py
@@ -16,7 +16,10 @@
 UNITS = 32
 FOLD = UNITS + UNITS // 2
 KINDS = 3
-SENT = F32
+FAR = 12
+NEAR = 7
+SUMS = ((0, 4, -8, -1), (1, 4, -16, 1), (1, 4, 8, 1), (0, 3, 15, -1), (0, 7, 7, -1), (1, 7, -7, 1))
+LAPS = ((0, 7, 0, -1), (1, 7, 0, 1), (0, 4, -12, -1), (1, 4, -12, 1), (0, 4, 12, -1), (1, 3, 12, 1))
 
 NT = (((1,), (1,)), ((), ()))
 NN = (((1,), (0,)), ((), ()))
@@ -36,10 +39,12 @@
 
 def kernel(
     experts, chips,
-    tok_ref, g_ref, id_ref, wg_ref, wu_ref, wd_ref, dy_ref,
+    tok_ref, g_ref, id_ref, wg_hbm, wu_hbm, wd_hbm, dy_ref,
     mixed_ref, gtok_ref, gwg_ref, gwu_ref, gwd_ref,
-    out_slots, in_slots, ret_slots, back_slots, xt, wt, wm, part, gath, acc_out, acc_back,
-    disp_s, disp_r, ret_s, ret_r, mate_s, mate_r, rs_s, rs_r, ag_s, ag_r, am_s, am_r,
+    wg_ref, wu_ref, wd_ref,
+    out_slots, in_slots, ret_slots, back_slots, xt, wt, wm, part, far_out, far_in, gath, acc_out, acc_back,
+    disp_s, disp_r, ret_s, ret_r, mate_s, mate_r, rs_s, rs_r, far_s, far_r, ag_s, ag_r, ax_s, ax_r, am_s, am_r,
+    load_s,
 ):
     e = lax.axis_index("expert")
     t = lax.axis_index("tensor")
@@ -47,8 +52,13 @@
     pad = FULL // experts
     slot = 192 // experts
     depth = wg_ref.shape[0]
-    half = chips // 2
     weights = (wg_ref, wu_ref, wd_ref)
+    loads = [
+        pltpu.make_async_copy(src, dst, load_s.at[k])
+        for k, (src, dst) in enumerate(zip((wg_hbm, wu_hbm, wd_hbm), weights))
+    ]
+    for load in loads:
+        load.start()
 
     def at_chip(k):
         return lax.rem(k + 2 * chips, chips)
@@ -57,9 +67,10 @@
     down_id = {"tensor": 2 * at_chip(z - 1) + c}
     mate_id = {"tensor": 2 * z + 1 - c}
     ring = (up_id, down_id)
+    far_ids = ({"tensor": 2 * at_chip(z + FAR) + c}, {"tensor": 2 * at_chip(z - FAR) + c})
 
     barrier = pltpu.get_barrier_semaphore()
-    for peer in (up_id, down_id, mate_id):
+    for peer in (up_id, down_id, mate_id, *far_ids):
         pl.semaphore_signal(barrier, inc=1, device_id=peer, device_id_type=MESH)
 
     def greet(i, _):
@@ -84,7 +95,7 @@
     out_slots[:, :, :LANES] = x_slots.reshape(experts, pad, LANES)
     out_slots[:, :, LANES:] = dy_slots.reshape(experts, pad, LANES)
 
-    pl.semaphore_wait(barrier, experts + 2)
+    pl.semaphore_wait(barrier, experts + 4)
 
     def leave(src, dst, send, recv, i):
         peer = lax.rem(e + i, experts)
@@ -138,6 +149,7 @@
             wt[k, pl.ds(2 * i, 2)] = block.reshape(2, 2, UNITS, LANES)
             return 0
 
+        loads[k].wait()
         lax.fori_loop(0, chips // 2, turn, 0)
         mate_weights(k).start()
 
@@ -174,46 +186,71 @@
             sums.append(jnp.concatenate([r[:, :LANES], tail], axis=0))
         return sums
 
-    def hop(way, s, k):
-        return pltpu.make_async_remote_copy(
-            src_ref=part.at[way, s, k], dst_ref=part.at[way, s + 1, k],
-            send_sem=rs_s.at[way, s, k], recv_sem=rs_r.at[way, s, k],
-            device_id=ring[way], device_id_type=MESH,
-        )
-
-    mine = partial(at_chip(z + half))
-    for k in range(KINDS):
-        part[0, 0, k] = mine[k].astype(SENT)
-        hop(0, 0, k).start()
-    mine = partial(at_chip(z - half + 1))
-    for k in range(KINDS):
-        part[1, 0, k] = mine[k].astype(SENT)
-        hop(1, 0, k).start()
-
-    def rs_step(i, _):
-        ups = partial(at_chip(z + half - i))
-        for k in range(KINDS):
-            hop(0, i - 1, k).wait_recv()
-            part[0, i, k] = (part[0, i, k].astype(F32) + ups[k]).astype(SENT)
-            hop(0, i, k).start()
-
-        @pl.when(i > 1)
-        def _():
-            downs = partial(at_chip(z - half + i))
-            for k in range(KINDS):
-                hop(1, i - 2, k).wait_recv()
-                part[1, i - 1, k] = (part[1, i - 1, k].astype(F32) + downs[k]).astype(SENT)
-                hop(1, i - 1, k).start()
-
+    def hop(i, s, k):
+        return pltpu.make_async_remote_copy(
+            src_ref=part.at[i, s, k], dst_ref=part.at[i, s + 1, k],
+            send_sem=rs_s.at[i, s, k], recv_sem=rs_r.at[i, s, k],
+            device_id=ring[SUMS[i][0]], device_id_type=MESH,
+        )
+
+    def summed(i, s):
+        return partial(at_chip(z + SUMS[i][2] + SUMS[i][3] * s))
+
+    def far(h, k):
+        return pltpu.make_async_remote_copy(
+            src_ref=far_out.at[h, k], dst_ref=far_in.at[h, k],
+            send_sem=far_s.at[h, k], recv_sem=far_r.at[h, k],
+            device_id=far_ids[h], device_id_type=MESH,
+        )
+
+    for i in range(len(SUMS)):
+        mine = summed(i, 0)
+        for k in range(KINDS):
+            part[i, 0, k] = mine[k]
+            hop(i, 0, k).start()
+
+    def advance(i, s):
+        mine = summed(i, s)
+        for k in range(KINDS):
+            hop(i, s - 1, k).wait_recv()
+            part[i, s, k] += mine[k]
+            hop(i, s, k).start()
+
+    def rs_step(s, _):
+        for i in range(len(SUMS)):
+            if SUMS[i][1] > 3:
+                advance(i, s)
+            else:
+                pl.when(s < SUMS[i][1])(functools.partial(advance, i, s))
         return 0
 
-    lax.fori_loop(1, half, rs_step, 0)
+    lax.fori_loop(1, 4, rs_step, 0)
+    for h, (one, two) in enumerate(((2, 3), (0, 1))):
+        mine = partial(at_chip(z + FAR - 2 * FAR * h))
+        for k in range(KINDS):
+            for i in (one, two):
+                hop(i, SUMS[i][1] - 1, k).wait_recv()
+            far_out[h, k] = (
+                part[one, SUMS[one][1], k] + part[two, SUMS[two][1], k] + mine[k]
+            ).astype(BF16)
+            far(h, k).start()
+
+    def rs_late(s, _):
+        advance(4, s)
+        advance(5, s)
+        return 0
+
+    lax.fori_loop(4, NEAR, rs_late, 0)
     own = partial(z)
     total = []
     for k in range(KINDS):
-        hop(0, half - 1, k).wait_recv()
-        hop(1, half - 2, k).wait_recv()
-        total.append(part[0, half, k].astype(F32) + part[1, half - 1, k].astype(F32) + own[k])
+        hop(4, NEAR - 1, k).wait_recv()
+        hop(5, NEAR - 1, k).wait_recv()
+        total.append(part[4, NEAR, k] + part[5, NEAR, k] + own[k])
+    for k in range(KINDS):
+        for h in range(2):
+            far(h, k).wait_recv()
+            total[k] += far_in[h, k].astype(F32)
     gate, up, d_hidden = total
     sigma = jax.nn.sigmoid(gate)
     active = gate * sigma
@@ -221,40 +258,53 @@
     gath[z, c, 1] = (d_hidden * up * sigma * (1.0 + gate * (1.0 - sigma))).astype(BF16)
     gath[z, c, 2] = (d_hidden * active).astype(BF16)
 
-    def lap(way, s, k):
-        origin = at_chip(z - s) if way == 0 else at_chip(z + s)
+    def lap(i, s, k):
+        origin = at_chip(z + LAPS[i][2] + LAPS[i][3] * s)
         return pltpu.make_async_remote_copy(
             src_ref=gath.at[origin, c, k], dst_ref=gath.at[origin, c, k],
-            send_sem=ag_s.at[way, s, k], recv_sem=ag_r.at[way, s, k],
-            device_id=ring[way], device_id_type=MESH,
-        )
-
-    def lap_in(way, s, k):
-        origin = at_chip(z - s - 1) if way == 0 else at_chip(z + s + 1)
+            send_sem=ag_s.at[i, s, k], recv_sem=ag_r.at[i, s, k],
+            device_id=ring[LAPS[i][0]], device_id_type=MESH,
+        )
+
+    def lap_from(i, s):
+        return at_chip(z - 1 + 2 * LAPS[i][0] + LAPS[i][2] + LAPS[i][3] * s)
+
+    def lap_in(i, s, k):
+        origin = lap_from(i, s)
         return pltpu.make_async_remote_copy(
             src_ref=gath.at[origin, c, k], dst_ref=gath.at[origin, c, k],
-            send_sem=ag_s.at[way, s, k], recv_sem=ag_r.at[way, s, k],
-            device_id=ring[way], device_id_type=MESH,
-        )
-
-    def across(origin, k):
+            send_sem=ag_s.at[i, s, k], recv_sem=ag_r.at[i, s, k],
+            device_id=ring[LAPS[i][0]], device_id_type=MESH,
+        )
+
+    def leap(h, k, arriving):
+        origin = at_chip(z - FAR + 2 * FAR * h) if arriving else z
         return pltpu.make_async_remote_copy(
             src_ref=gath.at[origin, c, k], dst_ref=gath.at[origin, c, k],
-            send_sem=am_s.at[origin, k], recv_sem=am_r.at[origin, k],
+            send_sem=ax_s.at[h, k], recv_sem=ax_r.at[h, k],
+            device_id=far_ids[h], device_id_type=MESH,
+        )
+
+    def across(origin):
+        return pltpu.make_async_remote_copy(
+            src_ref=gath.at[origin, c], dst_ref=gath.at[origin, c],
+            send_sem=am_s.at[origin], recv_sem=am_r.at[origin],
             device_id=mate_id, device_id_type=MESH,
         )
 
-    def across_in(origin, k):
-        return pltpu.make_async_remote_copy(
-            src_ref=gath.at[origin, 1 - c, k], dst_ref=gath.at[origin, 1 - c, k],
-            send_sem=am_s.at[origin, k], recv_sem=am_r.at[origin, k],
+    def across_in(origin):
+        return pltpu.make_async_remote_copy(
+            src_ref=gath.at[origin, 1 - c], dst_ref=gath.at[origin, 1 - c],
+            send_sem=am_s.at[origin], recv_sem=am_r.at[origin],
             device_id=mate_id, device_id_type=MESH,
         )
 
     for k in range(KINDS):
+        leap(0, k, False).start()
+        leap(1, k, False).start()
         lap(0, 0, k).start()
         lap(1, 0, k).start()
-        across(z, k).start()
+    across(z).start()
 
     acc_out[...] = jnp.zeros_like(acc_out)
     acc_back[...] = jnp.zeros_like(acc_back)
@@ -265,8 +315,7 @@
     def use(pair):
         first_chip = at_chip(z - odd + 2 * pair)
         for i in range(2):
-            for k in range(KINDS):
-                across_in(first_chip + i, k).wait_recv()
+            across_in(first_chip + i).wait_recv()
         panel = []
         for k in range(KINDS):
             rows = []
@@ -296,39 +345,56 @@
         gwu_ref[:, cols] = dot(x_panel, d_up, NT).astype(BF16)
         gwd_ref[:, cols] = dot(dy_panel, hidden, NT).astype(BF16)
 
-    def forward(s):
-        for k in range(KINDS):
-            lap_in(0, s, k).wait_recv()
-
-            @pl.when(s < half - 1)
+    def forward(i, s):
+        last = LAPS[i][1] - 1
+        for k in range(KINDS):
+            lap_in(i, s, k).wait_recv()
+
+            @pl.when(s < last)
             def _():
-                lap(0, s + 1, k).start()
-
-            across(at_chip(z - s - 1), k).start()
-
-            @pl.when(s < half - 1)
-            def _():
-                lap_in(1, s, k).wait_recv()
-
-                @pl.when(s < half - 2)
-                def _():
-                    lap(1, s + 1, k).start()
-
-                across(at_chip(z + s + 1), k).start()
-
-    forward(0)
-    forward(1)
-
-    def ag_step(j, _):
-        forward(2 * j)
-        use(j - 1 + odd)
-        forward(2 * j + 1)
-        use(odd - j)
+                lap(i, s + 1, k).start()
+
+        across(lap_from(i, s)).start()
+
+    def use_all(pairs):
+        def body(i, _):
+            pair = pairs[-1]
+            for j in range(len(pairs) - 1):
+                pair = jnp.where(i == j, pairs[j], pair)
+            use(pair)
+            return 0
+
+        lax.fori_loop(0, len(pairs), body, 0)
+
+    def near_step(s, _):
+        forward(0, s)
+        forward(1, s)
         return 0
 
-    lax.fori_loop(1, half // 2, ag_step, 0)
-    use(half // 2 - 1 + odd)
-    use(odd - half // 2)
+    lax.fori_loop(0, 3, near_step, 0)
+    use_all((0, 1, -1))
+    for h in range(2):
+        for k in range(KINDS):
+            leap(h, k, True).wait_recv()
+            lap(2 + 2 * h, 0, k).start()
+            lap(3 + 2 * h, 0, k).start()
+        across(at_chip(z - FAR + 2 * FAR * h)).start()
+
+    def ag_step(s):
+        forward(0, s + 3)
+        forward(1, s + 3)
+        for i in range(2, len(LAPS)):
+            if s < LAPS[i][1]:
+                forward(i, s)
+
+    ag_step(0)
+    use_all((6, -6))
+    ag_step(1)
+    use_all((2, -2))
+    ag_step(2)
+    use_all((5, -5, 7, -7, 6 * odd - 3))
+    ag_step(3)
+    use_all((3 - 6 * odd, 4, -4, -8))
 
     def folded(acc):
         a = acc[:, LANES:]
@@ -347,23 +413,21 @@
         mate_weights(k).wait_send()
     mate_rows.wait_send()
 
-    def drain(s, _):
-        for k in range(KINDS):
-            hop(0, s, k).wait_send()
-            lap(0, s, k).wait_send()
-
-            @pl.when(s < half - 1)
-            def _():
-                hop(1, s, k).wait_send()
-                lap(1, s, k).wait_send()
-
-        return 0
-
-    lax.fori_loop(0, half, drain, 0)
+    for h in range(2):
+        for k in range(KINDS):
+            far(h, k).wait_send()
+            leap(h, k, False).wait_send()
+    for chains, sent in ((SUMS, hop), (LAPS, lap)):
+        for i in range(len(chains)):
+            def drain(s, _, i=i, sent=sent):
+                for k in range(KINDS):
+                    sent(i, s, k).wait_send()
+                return 0
+
+            lax.fori_loop(0, chains[i][1], drain, 0)
 
     def drain_across(o, _):
-        for k in range(KINDS):
-            across(o, k).wait_send()
+        across(o).wait_send()
         return 0
 
     lax.fori_loop(0, chips, drain_across, 0)
@@ -375,40 +439,59 @@
     all_sent(*homeward)
 
 
+def hand_on(*refs):
+    for src, dst in zip(refs[:5], refs[5:]):
+        dst[...] = src[...]
+
+
 def local(experts, chips, tokens, gate_weights, expert_ids, w_gate, w_up, w_down, grad_out):
     depth, width = w_gate.shape[1:]
     pad = FULL // experts
-    half = chips // 2
     dma = pltpu.SemaphoreType.DMA
     slots = pltpu.VMEM((experts, pad, FULL), BF16)
     rows = jax.ShapeDtypeStruct((depth, LANES), BF16)
     grads = jax.ShapeDtypeStruct((depth, width), BF16)
     vmem = pl.BlockSpec(memory_space=pltpu.VMEM)
-    mixed, grad_tokens, gwg, gwu, gwd = pl.pallas_call(
+    results = pl.pallas_call(
         functools.partial(kernel, experts, chips),
         out_shape=(rows, rows, grads, grads, grads),
-        in_specs=[vmem] * 7,
+        in_specs=[vmem] * 3 + [pl.BlockSpec(memory_space=pl.ANY)] * 3 + [vmem],
         out_specs=(vmem,) * 5,
         scratch_shapes=[
+            pltpu.VMEM((depth, width), BF16),
+            pltpu.VMEM((depth, width), BF16),
+            pltpu.VMEM((depth, width), BF16),
             slots, slots, slots, slots,
             pltpu.VMEM((2, 2, LANES, FULL), BF16),
             pltpu.VMEM((KINDS, chips, 2, UNITS, LANES), BF16),
             pltpu.VMEM((KINDS, chips, UNITS, LANES), BF16),
-            pltpu.VMEM((2, half + 1, KINDS, FOLD, LANES), SENT),
+            pltpu.VMEM((len(SUMS), NEAR + 1, KINDS, FOLD, LANES), F32),
+            pltpu.VMEM((2, KINDS, FOLD, LANES), BF16),
+            pltpu.VMEM((2, KINDS, FOLD, LANES), BF16),
             pltpu.VMEM((chips, 2, KINDS, FOLD, LANES), BF16),
             pltpu.VMEM((depth, FULL), F32),
             pltpu.VMEM((depth, FULL), F32),
             dma((experts,)), dma((experts,)), dma((experts,)), dma((experts,)),
             dma((KINDS + 1,)), dma((KINDS + 1,)),
-            dma((2, half, KINDS)), dma((2, half, KINDS)),
-            dma((2, half, KINDS)), dma((2, half, KINDS)),
-            dma((chips, KINDS)), dma((chips, KINDS)),
+            dma((len(SUMS), NEAR, KINDS)), dma((len(SUMS), NEAR, KINDS)),
+            dma((2, KINDS)), dma((2, KINDS)),
+            dma((len(LAPS), NEAR, KINDS)), dma((len(LAPS), NEAR, KINDS)),
+            dma((2, KINDS)), dma((2, KINDS)),
+            dma((chips,)), dma((chips,)),
+            dma((KINDS,)),
         ],
         compiler_params=pltpu.CompilerParams(
-            collective_id=0, has_side_effects=True, vmem_limit_bytes=40 * 2**20
+            collective_id=0, has_side_effects=True, vmem_limit_bytes=56 * 2**20
         ),
         name="routed_experts",
     )(tokens.T, gate_weights.T, expert_ids.T, w_gate[0], w_up[0], w_down[0].T, grad_out.T)
+    mixed, grad_tokens, gwg, gwu, gwd = pl.pallas_call(
+        hand_on,
+        out_shape=(rows, rows, grads, grads, grads),
+        in_specs=[vmem] * 5,
+        out_specs=(vmem,) * 5,
+        name="hand_on",
+    )(*results)
     return mixed.T, grad_tokens.T, gwg[None], gwu[None], gwd.T[None]
 
 

time: 152 us -> 124 us (0.82)
  Pallas kernels: 142 us -> 123 us
  local copies, waits for them, and re-layouts: 8.72 us -> 0 us
    pallas_call x1, Pallas kernels: 142 us -> 120 us  [local(): pl.pallas_call(functools.partial(kernel, experts, chips), out_shape=(rows...]
    unnamed x19 -> x0, local copies, waits for them, and re-layouts: 8.72 us -> none
    pallas_call x0 -> x1, Pallas kernels: none -> 2.45 us  [local(): pl.pallas_call(hand_on, out_shape=(rows, rows, grads, grads, grads), in_s...]
where the time goes in v2:
time: 124 us
  Pallas kernels  123 us (99%)
    pallas_call x1, Pallas kernels, local(): pl.pallas_call(functools.partial(kernel, experts, chips), out_shape=(rows...  120 us

profile of v2, /device:TPU:1, one launch (start us, length us, event | category | flops | bytes accessed | tf_op | source)
XLA Modules:
  0.0 123.5 jit_solution(6754014162148174915)
XLA Ops:
  0.6 120.4 %routed_experts.1 = (bf16[112,128]{1,0:T(8,128)(2,1)}, bf16[112,128]{1,0:T(8,128)(2,1)}, bf16[112,2048]{1,0:T(8,128)(2,1)}, bf16[112,2048]{1,0:T(8,128)(2,1)}, bf16[112,2048]{1,0:T(8,128)(2,1)}) custom-call(bf16[112,128]{1,0:T(8,128)(2,1)} %bitcast.19, bf16[1,128]{1,0:T(2,128)(2,1)} %bitcast.21, s32[1,128]{1,0:T(1,128)} %bitcast.22, ...), custom_call_target="tpu_custom_call" | custom-call | tf_op jit(solution)/shard_map/routed_experts/pallas_call | solution.py:455
  121.1 2.4 %hand_on.1 = (bf16[112,128]{1,0:T(8,128)(2,1)}, bf16[112,128]{1,0:T(8,128)(2,1)}, bf16[112,2048]{1,0:T(8,128)(2,1)}, bf16[112,2048]{1,0:T(8,128)(2,1)}, bf16[112,2048]{1,0:T(8,128)(2,1)}) custom-call(bf16[112,128]{1,0:T(8,128)(2,1)} %get-tuple-element.15.refs_0_, bf16[112,128]{1,0:T(8,128)(2,1)} %get-tuple-element.16.refs_1_, ...), custom_call_target="tpu_custom_call" | custom-call | tf_op jit(solution)/shard_map/hand_on/pallas_call | solution.py:488
